TPU v7x, 512 devices: a whole 4x8x8 slice. The times are simulated.
512 devices in a mesh: member: 8 (over z_hi, core), lat: 64 (over z_lo, x, y).
Axes of the slice: x: 4, y: 8, z: 8 (z_hi: 4, z_lo: 2; z = z_hi * 2 + z_lo), core: 2. Of those that a mesh axis runs over, the one named last changes fastest.
Arguments:
- members: float32 [8, 16, 512, 1440], P('member', None, 'lat'), may hold values from 0.1 to 160, as said below
- conductivity: float32 [16, 512, 1440], P(None, 'lat'), may hold values from 0.1 to 1
- weights: float32 [8], P('member'), may hold values from 0.25 to 4
Outputs:
- barycenter: float32 [16, 512, 1440], P('member', 'lat')
Inputs may be any that keep to these rules, and one draw needn't show every extreme that they name: `members`: positive humidity densities.
All inputs are finite; a program needn't handle non-finite values.
Results may differ from a plain program's by a relative error of at most 0.00002.
Values sent between devices are 32-bit elements; how exact they have to be, the bound alone decides.
A program may use at most 64 MiB of HBM per device.

v0:
```python
import functools

import jax
import jax.numpy as jnp
from jax import lax
from jax.experimental import pallas as pl
from jax.experimental.pallas import tpu as pltpu
from jax.sharding import PartitionSpec as P

MESH = pl.DeviceIdType.MESH
STEP = 0.16
PASSES = 3
LEV, ROWS, LON = 16, 8, 1440
HALF = LEV // 2
CHUNKS = 4
COLS = LON // CHUNKS
GHOST = 12
TILES = 3
HALO = 3 * PASSES
ALL = ROWS + 2 * HALO
OWN = HALO
INNER = ROWS + 4 * PASSES
LAST = 1408


def lanes():
    return lax.broadcasted_iota(jnp.int32, (8, 128), 1)


def lane_tiles(ref, lev):
    tiles = [ref[lev, :, pl.ds(128 * i, 128)] for i in range(11)]
    return tiles + [jnp.concatenate([ref[lev, :, pl.ds(LAST, LON - LAST)], tiles[0][:, : 128 - (LON - LAST)]], axis=1)]


def chunk_tile(tiles, part, t):
    lane = lanes()
    start = COLS * part - GHOST
    shift = start % 128
    at = shift + 3 * lane + t
    if part == 0:
        window = [tiles[11], tiles[0], tiles[1], tiles[2]]
        index = jnp.where(at < 128, at - 96, at % 128)
        edges = [128, 256, 384]
    else:
        window = [tiles[start // 128 + i] for i in range(4)]
        index = at % 128
        edges = [128, 256, 384]
        if part == CHUNKS - 1:
            window.append(tiles[0])
            wrap = LON - 128 * (start // 128)
            index = jnp.where(at >= wrap, at - wrap, index)
            edges.append(wrap)
    value = jnp.take_along_axis(window[0], index, axis=1)
    for piece, edge in zip(window[1:], edges):
        value = jnp.where(at >= edge, jnp.take_along_axis(piece, index, axis=1), value)
    return value


def joined_tile(chunks, index):
    lane = lanes()
    result = None
    for part in range(CHUNKS):
        low, high = COLS * part, COLS * (part + 1)
        if low >= 128 * (index + 1) or high <= 128 * index:
            continue
        column = 128 * index + lane - low + GHOST
        source = jnp.clip(column // 3, 0, 127)
        kind = column % 3
        pieces = [jnp.take_along_axis(chunks[part][t], source, axis=1) for t in range(TILES)]
        value = jnp.where(kind == 0, pieces[0], jnp.where(kind == 1, pieces[1], pieces[2]))
        result = value if result is None else jnp.where(lane < low - 128 * index, result, value)
    return result


def kernel(
    members, conductivity, weights, out,
    xm, xc, sends, slabs, cond, cond_far, table_s, table_d, table_g, start, buf_a, buf_b,
    logs, logs_other, final, final_other, shares, gathered,
    weight_own, weight_in, weight_sum, weight_other, mass, column_in, plane_in,
    load_sem, local_sem, z_send, z_recv, w_send, w_recv, c_send, c_recv, y_send, y_recv, f_send, f_recv,
    s_send, s_recv, g_send, g_recv, t_send, t_recv, p_send, p_recv,
):
    me = lax.axis_index("member")
    lat = lax.axis_index("lat")
    zone, core = me // 2, lax.rem(me, 2)
    lat_count = lax.axis_size("lat")

    def zone_peer(k):
        return {"member": lax.rem(zone + k, CHUNKS) * 2 + core}

    def lat_peer(k):
        return {"lat": lax.rem(lat + k + lat_count, lat_count)}

    sibling = {"member": me + 1 - 2 * core}

    def column_peer(k):
        place = lax.rem(2 * zone + lat // 32 + k, 8)
        return {"member": place // 2 * 2 + core, "lat": lax.rem(place, 2) * 32 + lax.rem(lat, 32)}

    def plane_peer(k):
        return {"lat": lat // 32 * 32 + lax.rem(lat + k, 32)}

    load_m = pltpu.make_async_copy(members.at[0], xm, load_sem.at[1])
    load_c = pltpu.make_async_copy(conductivity, xc, load_sem.at[0])
    load_m.start()
    load_c.start()

    barrier = pltpu.get_barrier_semaphore()
    partners = [lat_peer(k) for k in (1, -1, 2, -2)] + [sibling] + [column_peer(k) for k in range(1, 8)]
    for partner in partners:
        pl.semaphore_signal(barrier, inc=1, device_id=partner, device_id_type=MESH)

    def greet(k, carry):
        pl.semaphore_signal(barrier, inc=1, device_id=plane_peer(k), device_id_type=MESH)
        return carry

    lax.fori_loop(1, 32, greet, 0)

    def remote(src, dst, send, recv, target):
        return pltpu.make_async_remote_copy(
            src_ref=src, dst_ref=dst, send_sem=send, recv_sem=recv, device_id=target, device_id_type=MESH
        )

    load_m.wait()

    def member_chunks(lev, carry):
        half = lev // HALF
        place = jnp.where(half == 0, lev, LEV - 1 - lev)
        tiles = lane_tiles(xm, lev)
        for part in range(CHUNKS):
            for t in range(TILES):
                sends[part, t, place, pl.ds(pl.multiple_of(8 * half, 8), 8), :] = chunk_tile(tiles, part, t)
        return carry

    lax.fori_loop(0, LEV, member_chunks, 0)
    load_c.wait()
    for part in range(CHUNKS):

        @pl.when(zone == part)
        def _(part=part):
            def cond_chunk(lev, carry):
                place = jnp.where(lev < HALF, lev, HALF + LEV - 1 - lev)
                tiles = lane_tiles(xc, lev)
                for t in range(TILES):
                    cond[1, place, t] = chunk_tile(tiles, part, t)
                return carry

            lax.fori_loop(0, LEV, cond_chunk, 0)

    weight_own[...] = jnp.full((8, 128), weights[0], jnp.float32)
    pl.semaphore_wait(barrier, len(partners) + 31)

    def block(b):
        return pl.ds(pl.multiple_of(16 * b, 16), 16)

    zone_copies = {
        (k, t): remote(
            sends.at[lax.rem(zone + k, CHUNKS), t], slabs.at[1, t, :, block(zone), :],
            z_send.at[k - 1, t], z_recv.at[k - 1, t], zone_peer(k),
        )
        for k in (1, 3, 2)
        for t in range(TILES)
    }
    for t in range(TILES):
        for k in (1, 3):
            zone_copies[k, t].start()
    mine = pltpu.make_async_copy(sends.at[zone], slabs.at[1, :, :, block(zone), :], local_sem.at[0])
    mine.start()

    own_half = pl.ds(pl.multiple_of(HALF * core, HALF), HALF)
    far_up = (cond.at[1, own_half, :, pl.ds(7, 1), :], cond_far.at[0, own_half, :, pl.ds(0, 1), :])
    far_down = (cond.at[1, own_half, :, pl.ds(0, 1), :], cond_far.at[1, own_half, :, pl.ds(0, 1), :])
    cond_copies = [
        remote(cond.at[1, own_half], cond.at[0, own_half], c_send.at[0], c_recv.at[0], lat_peer(1)),
        remote(cond.at[1, own_half], cond.at[2, own_half], c_send.at[1], c_recv.at[1], lat_peer(-1)),
        remote(*far_up, c_send.at[2], c_recv.at[2], lat_peer(2)),
        remote(*far_down, c_send.at[3], c_recv.at[3], lat_peer(-2)),
    ]
    for copy in cond_copies:
        copy.start()
    weight_copies = [
        remote(weight_own, weight_in.at[k - 1], w_send.at[k - 1], w_recv.at[k - 1], zone_peer(k)) for k in (1, 2, 3)
    ]
    for copy in weight_copies:
        copy.start()

    def forward(k, t):
        source = lax.rem(zone - k + CHUNKS, CHUNKS)
        part = slabs.at[1, t, :, block(source), :]
        return [
            remote(part, slabs.at[0, t, :, block(source), :], y_send.at[k, t, 0], y_recv.at[k, t, 0], lat_peer(1)),
            remote(part, slabs.at[2, t, :, block(source), :], y_send.at[k, t, 1], y_recv.at[k, t, 1], lat_peer(-1)),
        ]

    row_copies = []

    def pass_on(k, t):
        for copy in forward(k, t):
            copy.start()
            row_copies.append(copy)

    mine.wait()
    for t in range(TILES):
        pass_on(0, t)

    sub = lax.broadcasted_iota(jnp.int32, (8, 128), 0)
    even = sub % 2 == 0

    def spread(low, high):
        return jnp.where(even, jnp.broadcast_to(low, (8, 128)), jnp.broadcast_to(high, (8, 128)))

    def swap_halves(value):
        return jnp.where(even, pltpu.roll(value, 7, 0), pltpu.roll(value, 1, 0))

    def sides(value):
        west, east = pltpu.roll(value[2], 1, 1), pltpu.roll(value[0], 127, 1)
        return [west + value[1], value[0] + value[2], value[1] + east]

    def stencil(src, row, place):
        value = [src[row, place, t] for t in range(TILES)]
        total = sides(value)
        for t in range(TILES):
            total[t] = total[t] + (src[row - 1, place, t] + src[row + 1, place, t])
            if place > 0:
                total[t] = total[t] + src[row, place - 1, t]
            total[t] = total[t] + (src[row, place + 1, t] if place < HALF - 1 else swap_halves(value[t]))
        return value, total

    inside_low = jnp.where(lat == 0, 0.0, 1.0)
    inside_high = jnp.where(lat == lat_count - 1, 0.0, 1.0)
    far_low = jnp.where(lat <= 1, 0.0, 1.0)
    far_high = jnp.where(lat >= lat_count - 2, 0.0, 1.0)

    def root_rows(ref, source, count, first, inside):
        def body(row, carry):
            for place in range(HALF):
                for t in range(TILES):
                    low = ref[source, place, t, pl.ds(row, 1), :]
                    high = ref[source, HALF + place, t, pl.ds(row, 1), :]
                    table_s[first + row, place, t] = jnp.sqrt(spread(low, high)) * inside
            return carry

        lax.fori_loop(0, count, body, 0)

    def table_rows(low, high):
        def body(row, carry):
            for place in range(HALF):
                value, total = stencil(table_s, row, place)
                for t in range(TILES):
                    table_d[row, place, t] = 1.0 - STEP * (value[t] * total[t])
                    table_g[row, place, t] = STEP * (value[t] * value[t])
            return carry

        lax.fori_loop(low, high, body, 0)

    def start_rows(slab, first):
        def body(row, carry):
            for place in range(HALF):
                for t in range(TILES):
                    value = slabs[slab, t, place, pl.ds(row, 8, stride=8), :]
                    start[first + row, place, t] = value * table_s[first + row, place, t]
            return carry

        lax.fori_loop(0, ROWS, body, 0)

    root_rows(cond, 1, ROWS, OWN, 1.0)
    for copy in cond_copies:
        copy.wait()
    hand_copies = [
        remote(cond.at[0, own_half], cond.at[0, own_half], c_send.at[4], c_recv.at[4], sibling),
        remote(cond.at[2, own_half], cond.at[2, own_half], c_send.at[5], c_recv.at[5], sibling),
        remote(cond_far.at[:, own_half], cond_far.at[:, own_half], c_send.at[6], c_recv.at[6], sibling),
    ]
    for copy in hand_copies:
        copy.start()
    for k in (1, 3):
        zone_copies[k, 0].wait_recv()
        pass_on(k, 0)
    for t in range(TILES):
        zone_copies[2, t].start()
    for copy in hand_copies:
        copy.wait()
    root_rows(cond, 0, ROWS, OWN - ROWS, inside_low)
    root_rows(cond, 2, ROWS, OWN + ROWS, inside_high)
    root_rows(cond_far, 0, 1, 0, far_low)
    root_rows(cond_far, 1, 1, ALL - 1, far_high)
    for k in (1, 3):
        zone_copies[k, 1].wait_recv()
        pass_on(k, 1)
    table_rows(1, ALL // 2)
    for k in (1, 3):
        zone_copies[k, 2].wait_recv()
        pass_on(k, 2)
    table_rows(ALL // 2, ALL - 1)
    for t in range(TILES):
        zone_copies[2, t].wait_recv()
        pass_on(2, t)
    start_rows(1, OWN)
    far_copies = [
        remote(start.at[OWN + ROWS - 1], start.at[0], f_send.at[0], f_recv.at[0], lat_peer(2)),
        remote(start.at[OWN], start.at[ALL - 1], f_send.at[1], f_recv.at[1], lat_peer(-2)),
    ]
    for copy in far_copies:
        copy.start()
    for copy in weight_copies:
        copy.wait()
    group = sub // 2
    weight = jnp.zeros((8, 128), jnp.float32)
    total_weight = weight_own[...]
    for k in range(CHUNKS):
        value = weight_own[...] if k == 0 else weight_in[k - 1]
        weight = jnp.where(group == lax.rem(zone - k + CHUNKS, CHUNKS), value, weight)
        if k > 0:
            total_weight = total_weight + value
    weight_sum[...] = total_weight

    for copy in row_copies:
        copy.wait_recv()
    start_rows(0, OWN - ROWS)
    start_rows(2, OWN + ROWS)
    for copy in far_copies:
        copy.wait_recv()
    for row, inside in ((0, far_low), (ALL - 1, far_high)):
        for place in range(HALF):
            for t in range(TILES):
                start[row, place, t] = start[row, place, t] * inside

    def heat(src, dst, index):
        low = (index - 1) // 2 * 2 + 1

        def rows(j, carry):
            for place in range(HALF):
                for r in range(4):
                    row = low + 4 * j + r
                    value, total = stencil(src, row, place)
                    for t in range(TILES):
                        dst[row, place, t] = table_d[row, place, t] * value[t] + table_g[row, place, t] * total[t]
            return carry

        lax.fori_loop(0, (ALL - 2 * low) // 4, rows, 0)

    def guarded(value):
        return jnp.where(value > 0.0, value, 1.0)

    upper = sub >= 4
    odd_pair = (sub // 2) % 2 == 1

    def fold(a, b, c, d):
        def halves(x, y):
            return jnp.where(upper, y, x) + pltpu.roll(jnp.where(upper, x, y), 4, 0)

        x, y = halves(a, c), halves(b, d)
        other = jnp.where(odd_pair, pltpu.roll(y, 2, 0), pltpu.roll(x, 6, 0))
        return jnp.where(odd_pair, y, x) + other

    def log_sums(row, q, t):
        return fold(*[weight * jnp.log(guarded(buf_a[row, 4 * q + j, t])) for j in range(4)])

    heat(start, buf_a, 1)
    heat(buf_a, buf_b, 2)
    heat(buf_b, buf_a, 3)

    def first_logs(i, carry):
        for q in range(2):
            for t in range(TILES):
                logs[i, q, t] = log_sums(i + PASSES, q, t)
        return carry

    mid = INNER // 2
    sibling_copies = [
        remote(weight_sum, weight_other, s_send.at[0], s_recv.at[0], sibling),
        remote(logs.at[pl.ds(0, mid)], logs_other.at[pl.ds(0, mid)], s_send.at[1], s_recv.at[1], sibling),
        remote(logs.at[pl.ds(mid, mid)], logs_other.at[pl.ds(mid, mid)], s_send.at[2], s_recv.at[2], sibling),
    ]
    sibling_copies[0].start()
    lax.fori_loop(0, mid, first_logs, 0)
    sibling_copies[1].start()
    lax.fori_loop(mid, INNER, first_logs, 0)
    sibling_copies[2].start()
    sibling_copies[0].wait()
    inverse = 1.0 / (weight_sum[...] + weight_other[...])

    def rescale(i, carry):
        row = i + PASSES
        for q in range(2):
            for t in range(TILES):
                logs_other[i, q, t] = jnp.exp((logs[i, q, t] + logs_other[i, q, t]) * inverse)
        for place in range(HALF):
            q, j = place // 4, place % 4
            for t in range(TILES):
                power = spread(logs_other[i, q, t, pl.ds(2 * j, 1), :], logs_other[i, q, t, pl.ds(2 * j + 1, 1), :])
                buf_b[row, place, t] = table_s[row, place, t] * power / guarded(buf_a[row, place, t])
        return carry

    sibling_copies[1].wait()
    lax.fori_loop(0, mid, rescale, 0)
    sibling_copies[2].wait()
    lax.fori_loop(mid, INNER, rescale, 0)
    heat(buf_b, buf_a, 4)
    heat(buf_a, buf_b, 5)
    heat(buf_b, buf_a, 6)

    def ratio(row, carry):
        for place in range(HALF):
            for t in range(TILES):
                top = start[row, place, t] * table_s[row, place, t]
                buf_b[row, place, t] = top / guarded(buf_a[row, place, t])
        return carry

    lax.fori_loop(2 * PASSES, ALL - 2 * PASSES, ratio, 0)
    heat(buf_b, buf_a, 7)
    heat(buf_a, buf_b, 8)
    heat(buf_b, buf_a, 9)

    def second_logs(i, carry):
        for q in range(2):
            for t in range(TILES):
                final[t, q, pl.ds(pl.multiple_of(8 * i, 8), 8), :] = log_sums(i + OWN, q, t)
        return carry

    lax.fori_loop(0, ROWS, second_logs, 0)
    final_copy = remote(final, final_other, s_send.at[3], s_recv.at[3], sibling)
    final_copy.start()
    final_copy.wait()
    valid = []
    for t in range(TILES):
        at = 3 * lanes() + t
        valid.append((at >= GHOST) & (at < GHOST + COLS))
    summed = jnp.zeros((8, 128), jnp.float32)
    for lev in range(LEV):
        half, place = (0, lev) if lev < HALF else (1, LEV - 1 - lev)
        across = pl.ds(2 * (place % 4) + half, 8, stride=8)
        for t in range(TILES):
            value = jnp.exp((final[t, place // 4, across, :] + final_other[t, place // 4, across, :]) * inverse)
            value = value * lax.rsqrt(cond[1, HALF * half + place, t])
            summed = summed + jnp.where(valid[t], value, 0.0)
            shares[lev // 4, lev // 2 % 2, lev % 2, t] = value

    mass[0] = summed
    column_copies = [
        remote(mass.at[0], column_in.at[k - 1], t_send.at[k - 1], t_recv.at[k - 1], column_peer(k)) for k in range(1, 8)
    ]
    for copy in column_copies:
        copy.start()
    share_copies = [
        remote(
            shares.at[lax.rem(zone + k, CHUNKS), core], gathered.at[zone], g_send.at[k - 1], g_recv.at[k - 1],
            zone_peer(k),
        )
        for k in (1, 2, 3)
    ]
    for copy in share_copies:
        copy.start()
    gathered[zone] = shares[zone, core]
    for k, copy in enumerate(column_copies):
        copy.wait()
        summed = summed + column_in[k]

    mass[1] = summed

    def plane_copy(k):
        return remote(mass.at[1], plane_in.at[k - 1], p_send.at[k - 1], p_recv.at[k - 1], plane_peer(k))

    def send_plane(k, carry):
        plane_copy(k).start()
        return carry

    lax.fori_loop(1, 32, send_plane, 0)
    for copy in share_copies:
        copy.wait()
    joined = []
    for i in range(2):
        chunks = [[gathered[part, i, t] for t in range(TILES)] for part in range(CHUNKS)]
        joined.append([joined_tile(chunks, index) for index in range(12)])
    for t in range(TILES):
        for k in (1, 2, 3):
            zone_copies[k, t].wait_send()
    for copy in row_copies + far_copies:
        copy.wait_send()

    def take_plane(k, value):
        plane_copy(k).wait()
        return value + plane_in[k - 1]

    summed = lax.fori_loop(1, 32, take_plane, summed)
    cells = LEV * ROWS * lat_count * LON
    scale = cells / jnp.sum(summed)
    for i in range(2):
        for index in range(11):
            out[i, :, pl.ds(128 * index, 128)] = joined[i][index] * scale
        out[i, :, pl.ds(LAST, LON - LAST)] = (joined[i][11] * scale)[:, : LON - LAST]


def local(members, conductivity, weights):
    vmem = functools.partial(pltpu.VMEM, dtype=jnp.float32)
    dma = pltpu.SemaphoreType.DMA
    tiled = (TILES, 8, 128)
    table = (ALL, HALF) + tiled
    return pl.pallas_call(
        kernel,
        name="barycenter",
        out_shape=jax.ShapeDtypeStruct((2, ROWS, LON), jnp.float32),
        in_specs=[
            pl.BlockSpec(memory_space=pl.ANY),
            pl.BlockSpec(memory_space=pl.ANY),
            pl.BlockSpec(memory_space=pltpu.SMEM),
        ],
        out_specs=pl.BlockSpec(memory_space=pltpu.VMEM),
        scratch_shapes=[
            vmem((LEV, ROWS, LON)),
            vmem((LEV, ROWS, LON)),
            vmem((CHUNKS, TILES, HALF, 16, 128)),
            vmem((3, TILES, HALF, 64, 128)),
            vmem((3, LEV) + tiled),
            vmem((2, LEV) + tiled),
            vmem(table), vmem(table), vmem(table),
            vmem(table), vmem(table), vmem(table),
            vmem((INNER, 2) + tiled),
            vmem((INNER, 2) + tiled),
            vmem((TILES, 2, 64, 128)),
            vmem((TILES, 2, 64, 128)),
            vmem((CHUNKS, 2, 2) + tiled),
            vmem((CHUNKS, 2) + tiled),
            vmem((8, 128)),
            vmem((3, 8, 128)),
            vmem((8, 128)),
            vmem((8, 128)),
            vmem((2, 8, 128)),
            vmem((7, 8, 128)),
            vmem((31, 8, 128)),
            dma((2,)), dma((1,)),
            dma((3, 3)), dma((3, 3)), dma((3,)), dma((3,)), dma((7,)), dma((7,)),
            dma((4, 3, 2)), dma((4, 3, 2)), dma((2,)), dma((2,)), dma((4,)), dma((4,)),
            dma((3,)), dma((3,)), dma((7,)), dma((7,)), dma((31,)), dma((31,)),
        ],
        compiler_params=pltpu.CompilerParams(
            collective_id=0, has_side_effects=True, vmem_limit_bytes=60 * 1024 * 1024
        ),
    )(members, conductivity, weights)


def solution(mesh):
    placed = (P("member", None, "lat", None), P(None, "lat", None), P("member"))
    return jax.shard_map(
        local, mesh=mesh, in_specs=placed, out_specs=P("member", "lat", None), check_vma=False
    )
```

profile of v0, /device:TPU:1, one launch (start us, length us, event | category | flops | bytes accessed | tf_op | source)
XLA Modules:
  0.0 88.1 jit_solution(13894273808479180996)
XLA Ops:
  0.7 85.9 %barycenter.1 = f32[2,8,1440]{2,1,0:T(8,128)} custom-call(f32[1,16,8,1440]{3,2,1,0:T(8,128)} %members.1, f32[16,8,1440]{2,1,0:T(8,128)} %conductivity.1, f32[1]{0:T(128)S(6)} %copy.5.weights), custom_call_target="tpu_custom_call" | custom-call | tf_op jit(solution)/shard_map/barycenter/pallas_call | solution.py:499
  86.6 1.5 %copy.6 = f32[2,8,1440]{2,1,0:T(8,128)} copy(f32[2,8,1440]{2,1,0:T(8,128)} %barycenter.1) | data formatting | bytes 184320
where the time goes:
time: 88.6 us; the launch traced here: 88.1 us
  Pallas kernels  85.9 us (97%)
  local copies, waits for them, and re-layouts  1.54 us (2%)
    pallas_call x1, Pallas kernels, local(): pl.pallas_call(kernel, name='barycenter', out_shape=jax.ShapeDtypeStruct(...  85.9 us

commit v1 on v0

--- a/solution.py
+++ b/solution.py
@@ -74,10 +74,10 @@
 
 def kernel(
     members, conductivity, weights, out,
-    xm, xc, sends, slabs, cond, cond_far, table_s, table_d, table_g, start, buf_a, buf_b,
+    xm, xc, sends, slabs, relay, far, cond, cond_far, table_s, table_d, table_g, start, buf_a, buf_b,
     logs, logs_other, final, final_other, shares, gathered,
     weight_own, weight_in, weight_sum, weight_other, mass, column_in, plane_in,
-    load_sem, local_sem, z_send, z_recv, w_send, w_recv, c_send, c_recv, y_send, y_recv, f_send, f_recv,
+    load_sem, local_sem, r_recv, z_send, z_recv, w_send, w_recv, c_send, c_recv, y_send, y_recv, f_send, f_recv,
     s_send, s_recv, g_send, g_recv, t_send, t_recv, p_send, p_recv,
 ):
     me = lax.axis_index("member")
@@ -121,18 +121,129 @@
             src_ref=src, dst_ref=dst, send_sem=send, recv_sem=recv, device_id=target, device_id_type=MESH
         )
 
+    def block(b):
+        return pl.ds(pl.multiple_of(16 * b, 16), 16)
+
+    zone_copies = {
+        (k, t): remote(
+            sends.at[lax.rem(zone + k, CHUNKS), t], slabs.at[1, t, :, block(zone), :],
+            z_send.at[k - 1, t], z_recv.at[k - 1, t], zone_peer(k),
+        )
+        for k in (1, 3, 2)
+        for t in range(TILES)
+    }
+    local_copies = [
+        pltpu.make_async_copy(sends.at[zone, t], slabs.at[1, t, :, block(zone), :], local_sem.at[t])
+        for t in range(TILES)
+    ]
+    far_copies = []
+    edge_low, edge_high = lat == 0, lat == lat_count - 1
+    middle = lat_count // 2
+    relayed = {(0, 0): 0, (1, 0): 1, (3, 0): 2, (2, 0): 3, (1, 1): 4, (3, 2): 5}
+    step_up = (0, 1, middle - 1, edge_high, lat_count - 1, middle)
+    step_down = (1, -1, middle, edge_low, 0, middle - 1)
+
+    def row_copy(k, t, direction):
+        side, step = direction[0], direction[1]
+        source = lax.rem(zone - k + CHUNKS, CHUNKS)
+        part = sends.at[zone, t] if k == 0 else slabs.at[1, t, :, block(source), :]
+        return remote(
+            part, slabs.at[2 * side, t, :, block(source), :], y_send.at[k, t, side], y_recv.at[k, t, side], lat_peer(step)
+        )
+
+    def pass_on(k, t):
+        source = lax.rem(zone - k + CHUNKS, CHUNKS)
+        part = sends.at[zone, t] if k == 0 else slabs.at[1, t, :, block(source), :]
+        for direction in (step_up, step_down):
+            side, step, origin, edge, via, target = direction
+            if (k, t) in relayed:
+                index = relayed[k, t]
+
+                @pl.when((lat != origin) & jnp.logical_not(edge))
+                def _():
+                    row_copy(k, t, direction).start()
+
+                @pl.when(lat == origin)
+                def _():
+                    remote(part, relay.at[index], y_send.at[k, t, side], r_recv.at[index], {"lat": via}).start()
+
+            else:
+
+                @pl.when(jnp.logical_not(edge))
+                def _():
+                    row_copy(k, t, direction).start()
+
+    def relay_on(k, t):
+        index = relayed[k, t]
+        source = lax.rem(zone - k + CHUNKS, CHUNKS)
+        for direction in (step_up, step_down):
+            side, step, origin, edge, via, target = direction
+
+            @pl.when(edge)
+            def _():
+                onward = remote(
+                    relay.at[index], slabs.at[2 * side, t, :, block(source), :], y_send.at[k, t, side],
+                    y_recv.at[k, t, side], {"lat": target},
+                )
+                remote(part_of(t), relay.at[index], y_send.at[k, t, side], r_recv.at[index], {"lat": via}).wait_recv()
+                onward.start()
+
+    def part_of(t):
+        return sends.at[zone, t]
+
+    def rows_arrived():
+        for k in range(CHUNKS):
+            for t in range(TILES):
+
+                @pl.when(jnp.logical_not(edge_low))
+                def _():
+                    row_copy(k, t, step_up).wait_recv()
+
+                @pl.when(jnp.logical_not(edge_high))
+                def _():
+                    row_copy(k, t, step_down).wait_recv()
+
+    def rows_sent():
+        for k in range(CHUNKS):
+            for t in range(TILES):
+                for direction in (step_up, step_down):
+                    if (k, t) in relayed:
+                        row_copy(k, t, direction).wait_send()
+                    else:
+
+                        @pl.when(jnp.logical_not(direction[3]))
+                        def _():
+                            row_copy(k, t, direction).wait_send()
+
+    def pass_far(k):
+        source = lax.rem(zone - k + CHUNKS, CHUNKS)
+        for side, row, step in ((0, ROWS - 1, 2), (1, 0, -2)):
+            for half in range(2):
+                src = slabs.at[1, :, :, pl.ds(16 * source + 8 * half + row, 1), :]
+                dst = far.at[side, :, :, pl.ds(2 * source + half, 1), :]
+                copy = remote(src, dst, f_send.at[k, side, half], f_recv.at[k, side, half], lat_peer(step))
+                copy.start()
+                far_copies.append(copy)
+
     load_m.wait()
-
-    def member_chunks(lev, carry):
-        half = lev // HALF
-        place = jnp.where(half == 0, lev, LEV - 1 - lev)
-        tiles = lane_tiles(xm, lev)
-        for part in range(CHUNKS):
-            for t in range(TILES):
+    for t in range(TILES):
+
+        def member_chunks(lev, carry, t=t):
+            half = lev // HALF
+            place = jnp.where(half == 0, lev, LEV - 1 - lev)
+            tiles = lane_tiles(xm, lev)
+            for part in range(CHUNKS):
                 sends[part, t, place, pl.ds(pl.multiple_of(8 * half, 8), 8), :] = chunk_tile(tiles, part, t)
-        return carry
-
-    lax.fori_loop(0, LEV, member_chunks, 0)
+            return carry
+
+        lax.fori_loop(0, LEV, member_chunks, 0)
+        if t == 0:
+            pl.semaphore_wait(barrier, len(partners) + 31)
+        for k in (1, 3):
+            zone_copies[k, t].start()
+        pass_on(0, t)
+        local_copies[t].start()
+
     load_c.wait()
     for part in range(CHUNKS):
 
@@ -146,26 +257,6 @@
                 return carry
 
             lax.fori_loop(0, LEV, cond_chunk, 0)
-
-    weight_own[...] = jnp.full((8, 128), weights[0], jnp.float32)
-    pl.semaphore_wait(barrier, len(partners) + 31)
-
-    def block(b):
-        return pl.ds(pl.multiple_of(16 * b, 16), 16)
-
-    zone_copies = {
-        (k, t): remote(
-            sends.at[lax.rem(zone + k, CHUNKS), t], slabs.at[1, t, :, block(zone), :],
-            z_send.at[k - 1, t], z_recv.at[k - 1, t], zone_peer(k),
-        )
-        for k in (1, 3, 2)
-        for t in range(TILES)
-    }
-    for t in range(TILES):
-        for k in (1, 3):
-            zone_copies[k, t].start()
-    mine = pltpu.make_async_copy(sends.at[zone], slabs.at[1, :, :, block(zone), :], local_sem.at[0])
-    mine.start()
 
     own_half = pl.ds(pl.multiple_of(HALF * core, HALF), HALF)
     far_up = (cond.at[1, own_half, :, pl.ds(7, 1), :], cond_far.at[0, own_half, :, pl.ds(0, 1), :])
@@ -178,30 +269,28 @@
     ]
     for copy in cond_copies:
         copy.start()
+    for t in range(TILES):
+        zone_copies[2, t].start()
+    weight_own[...] = jnp.full((8, 128), weights[0], jnp.float32)
     weight_copies = [
         remote(weight_own, weight_in.at[k - 1], w_send.at[k - 1], w_recv.at[k - 1], zone_peer(k)) for k in (1, 2, 3)
     ]
     for copy in weight_copies:
         copy.start()
-
-    def forward(k, t):
-        source = lax.rem(zone - k + CHUNKS, CHUNKS)
-        part = slabs.at[1, t, :, block(source), :]
-        return [
-            remote(part, slabs.at[0, t, :, block(source), :], y_send.at[k, t, 0], y_recv.at[k, t, 0], lat_peer(1)),
-            remote(part, slabs.at[2, t, :, block(source), :], y_send.at[k, t, 1], y_recv.at[k, t, 1], lat_peer(-1)),
-        ]
-
-    row_copies = []
-
-    def pass_on(k, t):
-        for copy in forward(k, t):
-            copy.start()
-            row_copies.append(copy)
-
-    mine.wait()
-    for t in range(TILES):
-        pass_on(0, t)
+    for slab, edge in ((0, edge_low), (2, edge_high)):
+
+        @pl.when(edge)
+        def _(slab=slab):
+            def clear(place, carry):
+                for t in range(TILES):
+                    slabs[slab, t, place] = jnp.zeros((64, 128), jnp.float32)
+                return carry
+
+            lax.fori_loop(0, HALF, clear, 0)
+
+    for copy in local_copies:
+        copy.wait()
+    pass_far(0)
 
     sub = lax.broadcasted_iota(jnp.int32, (8, 128), 0)
     even = sub % 2 == 0
@@ -264,6 +353,9 @@
         lax.fori_loop(0, ROWS, body, 0)
 
     root_rows(cond, 1, ROWS, OWN, 1.0)
+    for k in (1, 3):
+        zone_copies[k, 0].wait_recv()
+        pass_on(k, 0)
     for copy in cond_copies:
         copy.wait()
     hand_copies = [
@@ -273,11 +365,10 @@
     ]
     for copy in hand_copies:
         copy.start()
+    relay_on(0, 0)
     for k in (1, 3):
-        zone_copies[k, 0].wait_recv()
-        pass_on(k, 0)
-    for t in range(TILES):
-        zone_copies[2, t].start()
+        zone_copies[k, 1].wait_recv()
+        pass_on(k, 1)
     for copy in hand_copies:
         copy.wait()
     root_rows(cond, 0, ROWS, OWN - ROWS, inside_low)
@@ -285,23 +376,22 @@
     root_rows(cond_far, 0, 1, 0, far_low)
     root_rows(cond_far, 1, 1, ALL - 1, far_high)
     for k in (1, 3):
-        zone_copies[k, 1].wait_recv()
-        pass_on(k, 1)
-    table_rows(1, ALL // 2)
-    for k in (1, 3):
         zone_copies[k, 2].wait_recv()
         pass_on(k, 2)
+        pass_far(k)
+        relay_on(k, 0)
+    table_rows(1, ALL // 2)
+    zone_copies[2, 0].wait_recv()
+    pass_on(2, 0)
+    relay_on(1, 1)
     table_rows(ALL // 2, ALL - 1)
-    for t in range(TILES):
+    for t in range(1, TILES):
         zone_copies[2, t].wait_recv()
         pass_on(2, t)
+    pass_far(2)
+    relay_on(3, 2)
+    relay_on(2, 0)
     start_rows(1, OWN)
-    far_copies = [
-        remote(start.at[OWN + ROWS - 1], start.at[0], f_send.at[0], f_recv.at[0], lat_peer(2)),
-        remote(start.at[OWN], start.at[ALL - 1], f_send.at[1], f_recv.at[1], lat_peer(-2)),
-    ]
-    for copy in far_copies:
-        copy.start()
     for copy in weight_copies:
         copy.wait()
     group = sub // 2
@@ -314,16 +404,15 @@
             total_weight = total_weight + value
     weight_sum[...] = total_weight
 
-    for copy in row_copies:
-        copy.wait_recv()
+    rows_arrived()
     start_rows(0, OWN - ROWS)
     start_rows(2, OWN + ROWS)
     for copy in far_copies:
         copy.wait_recv()
-    for row, inside in ((0, far_low), (ALL - 1, far_high)):
+    for side, row in ((0, 0), (1, ALL - 1)):
         for place in range(HALF):
             for t in range(TILES):
-                start[row, place, t] = start[row, place, t] * inside
+                start[row, place, t] = far[side, t, place] * table_s[row, place, t]
 
     def heat(src, dst, index):
         low = (index - 1) // 2 * 2 + 1
@@ -475,7 +564,8 @@
     for t in range(TILES):
         for k in (1, 2, 3):
             zone_copies[k, t].wait_send()
-    for copy in row_copies + far_copies:
+    rows_sent()
+    for copy in far_copies:
         copy.wait_send()
 
     def take_plane(k, value):
@@ -511,6 +601,8 @@
             vmem((LEV, ROWS, LON)),
             vmem((CHUNKS, TILES, HALF, 16, 128)),
             vmem((3, TILES, HALF, 64, 128)),
+            vmem((6, HALF, 16, 128)),
+            vmem((2, TILES, HALF, 8, 128)),
             vmem((3, LEV) + tiled),
             vmem((2, LEV) + tiled),
             vmem(table), vmem(table), vmem(table),
@@ -528,9 +620,9 @@
             vmem((2, 8, 128)),
             vmem((7, 8, 128)),
             vmem((31, 8, 128)),
-            dma((2,)), dma((1,)),
+            dma((2,)), dma((3,)), dma((6,)),
             dma((3, 3)), dma((3, 3)), dma((3,)), dma((3,)), dma((7,)), dma((7,)),
-            dma((4, 3, 2)), dma((4, 3, 2)), dma((2,)), dma((2,)), dma((4,)), dma((4,)),
+            dma((4, 3, 2)), dma((4, 3, 2)), dma((4, 2, 2)), dma((4, 2, 2)), dma((4,)), dma((4,)),
             dma((3,)), dma((3,)), dma((7,)), dma((7,)), dma((31,)), dma((31,)),
         ],
         compiler_params=pltpu.CompilerParams(

time: 88.6 us -> 76.3 us (0.86)
  Pallas kernels: 85.9 us -> 73.3 us
    pallas_call x1, Pallas kernels: 85.9 us -> 73.3 us  [local(): pl.pallas_call(kernel, name='barycenter', out_shape=jax.ShapeDtypeStruct(...]
where the time goes in v1:
time: 76.3 us; the launch traced here: 75.5 us
  Pallas kernels  73.3 us (96%)
  local copies, waits for them, and re-layouts  1.54 us (2%)
    pallas_call x1, Pallas kernels, local(): pl.pallas_call(kernel, name='barycenter', out_shape=jax.ShapeDtypeStruct(...  73.3 us
    unnamed x1, local copies, waits for them, and re-layouts  1.54 us

profile of v1, /device:TPU:1, one launch (start us, length us, event | category | flops | bytes accessed | tf_op | source)
XLA Modules:
  0.0 75.5 jit_solution(183089645275523448)
XLA Ops:
  0.7 73.3 %barycenter.1 = f32[2,8,1440]{2,1,0:T(8,128)} custom-call(f32[1,16,8,1440]{3,2,1,0:T(8,128)} %members.1, f32[16,8,1440]{2,1,0:T(8,128)} %conductivity.1, f32[1]{0:T(128)S(6)} %copy.5.weights), custom_call_target="tpu_custom_call" | custom-call | tf_op jit(solution)/shard_map/barycenter/pallas_call | solution.py:589
  74.0 1.5 %copy.6 = f32[2,8,1440]{2,1,0:T(8,128)} copy(f32[2,8,1440]{2,1,0:T(8,128)} %barycenter.1) | data formatting | bytes 184320
